TPU v7x, 32 devices: a whole 2x2x4 slice. The times are simulated.
32 devices in a mesh: stn: 4 (over y, x), tm: 8 (over z, core).
Axes of the slice: x: 2, y: 2, z: 4, core: 2. Of those that a mesh axis runs over, the one named last changes fastest.
Arguments:
- voltages: bfloat16 [512, 128, 4096], P('stn', 'tm'), may hold values from -52 to 52
- pfb_taps: float32 [16, 4096], replicated, may hold values from -1.5 to 1.5
- eq_gains: float32 [512, 2048], P('stn'), may hold values from 0.5 to 11
Outputs:
- visibilities: float32 [2048, 512, 512], P(('stn', 'tm'))
All inputs are finite; a program needn't handle non-finite values.
Results may differ from a plain program's by a relative error of at most 0.0014.
Values may be sent and summed in bfloat16 or wider, within the bound.
A program may use at most 448 MiB of HBM per device.

v0:
```python
import math

import jax
import jax.numpy as jnp
from jax import lax
from jax.sharding import PartitionSpec as P


def from_behind(value, axis, steps):
    count = lax.axis_size(axis)
    first, last = (max(0, -steps), min(count, count - steps))
    return lax.ppermute(value, axis, [(source, source + steps) for source in range(first, last)])


def cos_sin(numer, denom):
    angle = 2.0 * math.pi / denom * (numer % denom).astype(jnp.float32)
    return (jnp.cos(angle), jnp.sin(angle))


def transform(filtered, channels):
    inputs_dev, frames_dev, length = filtered.shape
    inner_len = 64
    outer_len = length // inner_len
    kept_upper = channels // outer_len
    row_count = inputs_dev * frames_dev
    highest = lax.Precision.HIGHEST
    arranged = filtered.reshape(row_count, outer_len, inner_len)
    freq_one = lax.broadcasted_iota(jnp.int32, (outer_len, outer_len), 0)
    time_one = lax.broadcasted_iota(jnp.int32, (outer_len, outer_len), 1)
    cos_one, sin_one = cos_sin(freq_one * time_one, outer_len)
    section_one = jnp.stack([cos_one, -sin_one])
    partial_ft = jnp.einsum("qka,Rab->qkbR", section_one, arranged, precision=highest)
    freq_twist = lax.broadcasted_iota(jnp.int32, (outer_len, inner_len), 0)
    time_twist = lax.broadcasted_iota(jnp.int32, (outer_len, inner_len), 1)
    twist_cos, twist_sin = cos_sin(freq_twist * time_twist, length)
    twist_table = jnp.stack([jnp.stack([twist_cos, twist_sin]), jnp.stack([-twist_sin, twist_cos])])
    freq_two = lax.broadcasted_iota(jnp.int32, (kept_upper, inner_len), 0)
    time_two = lax.broadcasted_iota(jnp.int32, (kept_upper, inner_len), 1)
    cos_two, sin_two = cos_sin(freq_two * time_two, inner_len)
    section_two = jnp.stack(
        [jnp.stack([cos_two, sin_two], axis=1), jnp.stack([-sin_two, cos_two], axis=1)]
    )
    combined = jnp.einsum("qjrb,rskb->qjksb", section_two, twist_table, precision=highest)
    spectrum = jnp.einsum("qjksb,skbR->qjkR", combined, partial_ft, precision=highest)
    return spectrum.reshape(2, channels, row_count)


def per_device(voltages, pfb_taps, eq_gains):
    tap_count = pfb_taps.shape[0]
    history_len = tap_count - 1
    inputs_dev, frames_dev, length = voltages.shape
    channels = eq_gains.shape[1]
    station_groups = lax.axis_size("stn")
    time_groups = lax.axis_size("tm")
    per_group = channels // (station_groups * time_groups)
    all_inputs = inputs_dev * station_groups
    all_frames = frames_dev * time_groups
    earlier = from_behind(voltages[:, frames_dev - history_len :, :], "tm", 1)
    extended = jnp.concatenate([earlier, voltages], axis=1).astype(jnp.float32)
    kernel = jnp.flip(pfb_taps, axis=0)[:, None, :]
    filtered = lax.conv_general_dilated(
        extended,
        kernel,
        (1,),
        "VALID",
        dimension_numbers=("NWC", "WIO", "NWC"),
        feature_group_count=length,
        precision=lax.Precision.HIGHEST,
    )
    spectrum = transform(filtered, channels)
    gains_turned = jnp.transpose(eq_gains)
    spectra = (
        spectrum.reshape(2, channels, inputs_dev, frames_dev) * gains_turned[None, :, :, None]
    ).astype(jnp.bfloat16)
    shaped = spectra.reshape(2, station_groups * time_groups, per_group, inputs_dev * frames_dev)
    turned = lax.all_to_all(shaped, ("stn", "tm"), split_axis=1, concat_axis=1, tiled=True)
    blocks = turned.reshape(2, station_groups, time_groups, per_group, inputs_dev, frames_dev)
    columns = jnp.transpose(blocks, (0, 3, 1, 4, 2, 5)).reshape(
        2, per_group, all_inputs, all_frames
    )
    swapped = jnp.stack([columns[1], -columns[0]])
    vis_real = jnp.einsum("rcnt,rcmt->cnm", columns, columns, preferred_element_type=jnp.float32)
    vis_imag = jnp.einsum("rcnt,rcmt->cnm", swapped, columns, preferred_element_type=jnp.float32)
    local_power = jnp.sum(jnp.diagonal(vis_real, axis1=1, axis2=2), axis=0)
    power = lax.psum(local_power, ("stn", "tm"))
    scale = lax.rsqrt(power / (all_frames * channels) + 1e-06)
    weight = scale[:, None] * scale[None, :] / all_frames
    row_ids = lax.broadcasted_iota(jnp.int32, (all_inputs, all_inputs), 0)
    col_ids = lax.broadcasted_iota(jnp.int32, (all_inputs, all_inputs), 1)
    lower = row_ids >= col_ids
    return jnp.where(lower[None], vis_real, vis_imag) * weight[None]


def solution(mesh):
    in_specs = (P("stn", "tm", None), P(), P("stn", None))
    out_specs = P(("stn", "tm"), None, None)
    return jax.shard_map(
        per_device, mesh=mesh, in_specs=in_specs, out_specs=out_specs, check_vma=False
    )
```

profile of v0, /device:TPU:10, one launch (start us, length us, event | category | flops | bytes accessed | tf_op | source)
XLA Modules:
  0.0 1406.1 jit_solution(4056926217263427299)
XLA Ops:
  0.0 14.7 %copy.48 = bf16[128,16,4096]{2,0,1:T(8,128)(2,1)S(1)} copy(bf16[128,16,4096]{2,1,0:T(8,128)(2,1)} %param.3) | data formatting | bytes 33554432 | tf_op args[0]
  14.7 5.7 copy-done
  20.5 6.2 slice.19
  35.2 6.8 copy.56
  42.0 7.8 mul.180
  49.9 27.9 %mul.181 = f32[32,64,2048]{1,0,2:T(8,128)} reshape(f32[2048,128,16]{0,2,1:T(8,128)} %mul.180) | data formatting | bytes 33554432 | tf_op jit(solution)/shard_map/mul | solution.py:73
  77.8 26.2 %copy.57 = f32[32,64,2048]{2,0,1:T(8,128)} copy(f32[32,64,2048]{1,0,2:T(8,128)} %mul.181) | data formatting | bytes 33554432 | tf_op jit(solution)/shard_map/mul | solution.py:73
  104.7 95.6 %collective-permute-done = bf16[128,15,4096]{2,0,1:T(8,128)(2,1)} collective-permute-done((bf16[128,15,4096]{2,0,1:T(8,128)(2,1)}, bf16[128,15,4096]{2,0,1:T(8,128)(2,1)}, u32[]{:S(2)}, u32[]{:S(2)}) %collective-permute-start) | collective-permute-done | bytes 15728672 | tf_op jit(solution)/shard_map/ppermute | solution.py:12
  200.4 44.3 %fusion.4 = f32[128,16,4096]{2,0,1:T(8,128)S(1)} fusion(bf16[128,16,4096]{2,0,1:T(8,128)(2,1)} %copy-done, bf16[128,15,4096]{2,0,1:T(8,128)(2,1)} %collective-permute-done, f32[16,1,4096]{2,0,1:T(8,128)S(1)} %bitcast.67), kind=kOutput, calls=%fused_computation.7 | convolution fusion | flops 1626865664 | bytes 66322432 | tf_op jit(solution)/shard_map/conv_general_dilated | solution.py:61
  244.7 35.5 %copy.51 = f32[128,16,4096]{2,1,0:T(8,128)} copy(f32[128,16,4096]{2,0,1:T(8,128)S(1)} %fusion.4) | data formatting | bytes 67108864 | tf_op jit(solution)/shard_map/conv_general_dilated | solution.py:61
  280.2 52.6 %reshape.233 = f32[2048,64,64]{2,1,0:T(8,128)} reshape(f32[128,16,4096]{2,1,0:T(8,128)} %copy.51) | data formatting | bytes 67108864 | tf_op jit(solution)/shard_map/reshape | solution.py:27
  332.8 51.1 %copy.70 = f32[2048,64,64,1]{0,1,3,2:T(8,128)} copy(f32[2048,64,64,1]{2,1,0,3:T(8,128)} %bitcast.1) | data formatting | bytes 67108864 | tf_op jit(solution)/shard_map/reshape | solution.py:27
  383.9 60.8 %convolution_bitcast_fusion.1 = f32[2,64,64,2048,1]{3,1,0,2,4:T(8,128)} fusion(f32[2048,64,64,1]{0,1,3,2:T(8,128)} %copy.70, f32[1,64,64]{2,1,0:T(8,128)S(1)} %copy-done.6, f32[1,64,64]{2,1,0:T(8,128)S(1)} %copy-done.7), kind=kOutput, calls=%fused_computation.12 | convolution fusion | flops 12884910080 | bytes 100696064 | tf_op jit(solution)/shard_map/qka,Rab->qkbR/dot_general | solution.py:32
  444.7 90.9 %fusion.3 = bf16[2,32,64,2048]{3,1,0,2:T(8,128)(2,1)} fusion(f32[2,32,64,2,64]{4,1,3,0,2:T(8,128)S(1)} %copy-done.2, f32[2,64,64,2048,1]{3,1,0,2,4:T(8,128)} %convolution_bitcast_fusion.1, f32[32,64,2048]{2,0,1:T(8,128)} %copy.57), kind=kOutput, calls=%fused_computation.6 | convolution fusion | flops 12901679104 | bytes 102760448 | tf_op jit(solution)/shard_map/qjksb,skbR->qjkR/dot_general | solution.py:44
  535.6 31.0 %copy.58 = bf16[2,32,64,2048]{3,0,2,1:T(2,128)(2,1)} copy(bf16[2,32,64,2048]{3,1,0,2:T(8,128)(2,1)} %fusion.3) | data formatting | bytes 33554432 | tf_op jit(solution)/shard_map/convert_element_type | solution.py:74
  566.6 6.1 all-to-all-start
  574.0 358.9 %all-to-all-done = bf16[2,32,64,2048]{3,0,2,1:T(2,128)(2,1)} async-done(((bf16[2,32,64,2048]{3,0,2,1:T(2,128)(2,1)}), bf16[2,32,64,2048]{3,0,2,1:T(2,128)(2,1)}, u32[]{:S(2)}, u32[]{:S(2)}) %all-to-all-start) | async-done | bytes 16777248 | tf_op jit(solution)/shard_map/all_to_all | solution.py:76
  932.9 46.9 %copy.59 = bf16[2,32,64,2048]{2,3,1,0:T(8,128)(2,1)} copy(bf16[2,32,64,2048]{3,0,2,1:T(2,128)(2,1)} %all-to-all-done) | data formatting | bytes 33554432 | tf_op jit(solution)/shard_map/all_to_all | solution.py:76
  979.8 45.5 %copy.60 = bf16[2,4,8,64,128,16]{4,5,2,1,3,0:T(8,128)(2,1)} copy(bf16[2,4,8,64,128,16]{3,5,4,2,1,0:T(8,128)(2,1)} %bitcast.62) | data formatting | bytes 33554432 | tf_op jit(solution)/shard_map/reshape | solution.py:77
  1025.2 9.3 fusion.44
  1034.6 11.6 copy.64
  1046.2 13.1 slice.15
  1059.3 12.0 copy.66
  1071.3 20.1 %copy.65 = bf16[1,64,4,128,8,16]{3,2,5,4,1,0:T(4,128)(2,1)} copy(bf16[1,64,4,128,8,16]{3,5,4,2,1,0:T(8,128)(2,1)} %get-tuple-element.6) | data formatting | bytes 16777216 | tf_op jit(solution)/shard_map/neg | solution.py:81
  1091.3 13.1 neg.47
  1104.4 11.7 copy.67
  1116.1 42.9 %copy.61 = bf16[2,64,4,128,8,16]{3,2,5,4,1,0:T(4,128)(2,1)} copy(bf16[2,64,4,128,8,16]{1,5,3,4,2,0:T(8,128)(2,1)} %bitcast.63) | data formatting | bytes 33554432 | tf_op jit(solution)/shard_map/transpose | solution.py:78
  1159.0 24.9 %reshape.235 = bf16[2,64,512,128]{2,3,1,0:T(8,128)(2,1)} reshape(bf16[2,64,4,128,8,16]{3,2,5,4,1,0:T(4,128)(2,1)} %copy.61) | data formatting | bytes 33554432 | tf_op jit(solution)/shard_map/reshape | solution.py:78
  1183.8 32.4 %convolution_bitcast_fusion = f32[64,512,512]{2,1,0:T(8,128)} fusion(bf16[2,64,512,128]{2,3,1,0:T(8,128)(2,1)} %reshape.235), kind=kOutput, calls=%fused_computation.11 | convolution fusion | flops 8589934592 | bytes 83886080 | tf_op jit(solution)/shard_map/rcnt,rcmt->cnm/dot_general | solution.py:82
  1216.3 87.7 %copy.69 = f32[64,512,512]{0,2,1:T(8,128)} copy(f32[64,512,512]{2,1,0:T(8,128)} %convolution_bitcast_fusion) | data formatting | bytes 134217728 | tf_op jit(solution)/shard_map/rcnt,rcmt->cnm/dot_general | solution.py:82
  1309.7 43.3 %psum.7 = f32[512]{0:T(512)S(1)} all-reduce(f32[512]{0:T(512)S(1)} %reduce_sum.9), channel_id=1, replica_groups=mesh['stn'=4,'tm'=8] {'stn','tm'}, use_global_device_ids=true, to_apply=%region_1.2 | all-reduce | flops 512 | bytes 4096 | tf_op jit(solution)/shard_map/psum | solution.py:85
  1353.2 52.7 %fusion = f32[64,512,512]{2,1,0:T(8,128)} fusion(f32[64,512,512]{2,1,0:T(8,128)} %convolution_bitcast_fusion, f32[512,512]{1,0:T(8,128)S(1)} %multiply_multiply_fusion, pred[512,512]{1,0:T(8,128)(4,1)S(1)} %copy-done.3, bf16[1,64,512,128]{3,2,0,1:T(8,128)(2,1)} %copy.67, bf16[1,64,512,128]{3,2,0,1:T(8,128)(2,1)} %copy.66, bf16[2,64,512,128]{2,3,1,0:T(8,128)(2,1)} %reshape.235), kind=kOutput, calls=%fused_computation.2 | convolution fusion | flops 8631877632 | bytes 169082880 | tf_op jit(solution)/shard_map/rcnt,rcmt->cnm/dot_general | solution.py:83
  (35 shorter events, 16.5 us)
Async XLA Ops:
  14.7 5.7 copy-start
  20.5 8.9 copy-start.5
  20.5 21.5 %copy-start.4 = (f32[128,2048]{1,0:T(8,128)S(1)}, f32[128,2048]{1,0:T(8,128)}, u32[]{:S(2)}) copy-start(f32[128,2048]{1,0:T(8,128)} %param.5) | copy-start | bytes 3145732
  26.6 173.7 %collective-permute-start = (bf16[128,15,4096]{2,0,1:T(8,128)(2,1)}, bf16[128,15,4096]{2,0,1:T(8,128)(2,1)}, u32[]{:S(2)}, u32[]{:S(2)}) collective-permute-start(bf16[128,15,4096]{2,0,1:T(8,128)(2,1)} %slice.19), channel_id=1, source_target_pairs={{0,1},{1,2},{2,3},{3,4},{4,5},{5,6},{6,7},{8,9},{9,10},{10,11},{11... | collective-permute-start | bytes 47185928 | tf_op jit(solution)/shard_map/ppermute | solution.py:12
  332.8 51.1 %copy-start.6 = (f32[1,64,64]{2,1,0:T(8,128)S(1)}, f32[1,64,64]{2,1,0:T(8,128)}, u32[]{:S(2)}) copy-start(f32[1,64,64]{2,1,0:T(8,128)} %get-tuple-element.15) | copy-start | bytes 49156
  332.8 51.1 %copy-start.7 = (f32[1,64,64]{2,1,0:T(8,128)S(1)}, f32[1,64,64]{2,1,0:T(8,128)}, u32[]{:S(2)}) copy-start(f32[1,64,64]{2,1,0:T(8,128)} %get-tuple-element.16) | copy-start | bytes 49156
  383.9 60.8 %copy-start.2 = (f32[2,32,64,2,64]{4,1,3,0,2:T(8,128)S(1)}, f32[2,32,64,2,64]{4,1,3,0,2:T(8,128)}, u32[]{:S(2)}) copy-start(f32[2,32,64,2,64]{4,1,3,0,2:T(8,128)} %copy.56) | copy-start | bytes 6291460
  566.6 366.3 %all-to-all-start = ((bf16[2,32,64,2048]{3,0,2,1:T(2,128)(2,1)}), bf16[2,32,64,2048]{3,0,2,1:T(2,128)(2,1)}, u32[]{:S(2)}, u32[]{:S(2)}) async-start(bf16[2,32,64,2048]{3,0,2,1:T(2,128)(2,1)} %copy.58), calls=%async_computation | async-start | bytes 33554432 | tf_op jit(solution)/shard_map/all_to_all | solution.py:76
  1216.3 87.7 %copy-start.1 = (s32[512,1]{0,1:T(1,128)S(1)}, s32[512,1]{0,1:T(1,128)}, u32[]{:S(2)}) copy-start(s32[512,1]{0,1:T(1,128)} %shift-left_or_fusion) | copy-start | bytes 6148
  1216.3 136.9 %copy-start.3 = (pred[512,512]{1,0:T(8,128)(4,1)S(1)}, pred[512,512]{1,0:T(8,128)(4,1)}, u32[]{:S(2)}) copy-start(pred[512,512]{1,0:T(8,128)(4,1)} %iota_compare_fusion) | copy-start | bytes 786436
where the time goes:
time: 1420 us; the launch traced here: 1410 us
  local copies, waits for them, and re-layouts  601 us (42%)
  waiting for transfers between devices  455 us (32%)
  matrix products  286 us (20%)
  blocking collectives  43.3 us (3%)
    all_to_all x1, waiting for transfers between devices, per_device(): lax.all_to_all(shaped, ('stn', 'tm'), split_axis=1, concat_axis=1, tiled=...  359 us
    reshape x2, local copies, waits for them, and re-layouts, transform(): arranged = filtered.reshape(row_count, outer_len, inner_len)  104 us
    ppermute x1, waiting for transfers between devices, from_behind(): lax.ppermute(value, axis, [(source, source + steps) for source in range(f...  95.6 us
    dot_general x1, matrix products, transform(): jnp.einsum('qjksb,skbR->qjkR', combined, partial_ft, precision=highest)  90.9 us
    dot_general x1, local copies, waits for them, and re-layouts, per_device(): jnp.einsum('rcnt,rcmt->cnm', columns, columns, preferred_element_type=jnp...  87.7 us
    mul x3, local copies, waits for them, and re-layouts, per_device(): spectrum.reshape(2, channels, inputs_dev, frames_dev)  61.9 us
    dot_general x1, matrix products, transform(): jnp.einsum('qka,Rab->qkbR', section_one, arranged, precision=highest)  60.8 us
    dot_general x1, matrix products, per_device(): jnp.einsum('rcnt,rcmt->cnm', swapped, columns, preferred_element_type=jnp...  52.7 us
  transfers between devices with their start and end apart: 2, of which 2 were waited for; matrix products, arithmetic and copies ran while one was open for 6% of the time, Pallas kernels for 0%

commit v1 on v0

--- a/solution.py
+++ b/solution.py
@@ -1,8 +1,13 @@
+import functools
 import math
 
 import jax
 import jax.numpy as jnp
+import ml_dtypes
+import numpy as np
 from jax import lax
+from jax.experimental import pallas as pl
+from jax.experimental.pallas import tpu as pltpu
 from jax.sharding import PartitionSpec as P
 
 
@@ -91,9 +96,307 @@
     return jnp.where(lower[None], vis_real, vis_imag) * weight[None]
 
 
+OUTER = 16
+INNER = 256
+NT = (((1,), (1,)), ((), ()))
+TN = (((0,), (0,)), ((), ()))
+
+
+def split_pair(table):
+    high = table.astype(ml_dtypes.bfloat16)
+    low = (table - high.astype(np.float64)).astype(ml_dtypes.bfloat16)
+    return np.stack([high, low])
+
+
+def dft_tables(length):
+    def parts(residue):
+        freq = residue + OUTER * np.arange(INNER // 2)[:, None]
+        angle = -2.0 * np.pi / length * ((freq * np.arange(INNER)[None, :]) % length)
+        return np.cos(angle), np.sin(angle)
+
+    pairs = []
+    for residue in range(1, OUTER // 2):
+        c, s = parts(residue)
+        cm, sm = parts(OUTER - residue)
+        pairs.append(np.block([[c, -s], [s, c], [cm, sm], [sm, -cm]]))
+    singles = [np.concatenate(parts(residue)) for residue in (0, OUTER // 2)]
+    return split_pair(np.stack(pairs)), split_pair(np.stack(singles))
+
+
+def real_dft16(x):
+    r = math.sqrt(0.5)
+    s = [x[n] + x[n + 8] for n in range(8)]
+    d = [x[n] - x[n + 8] for n in range(8)]
+    t = [s[n] + s[n + 4] for n in range(4)]
+    u = [s[n] - s[n + 4] for n in range(4)]
+    even, odd = t[0] + t[2], t[1] + t[3]
+    minus, plus = (u[1] - u[3]) * r, (u[1] + u[3]) * r
+    out = {
+        0: (even + odd, None),
+        8: (even - odd, None),
+        4: (t[0] - t[2], t[3] - t[1]),
+        2: (u[0] + minus, -plus - u[2]),
+        6: (u[0] - minus, u[2] - plus),
+    }
+    e = [None] + [d[n] - d[8 - n] for n in range(1, 4)]
+    g = [None] + [d[n] + d[8 - n] for n in range(1, 4)]
+    for k in (1, 3, 5, 7):
+        re, im = d[0], d[4] * (-math.sin(math.pi * k / 2))
+        for n in range(1, 4):
+            re = re + e[n] * math.cos(math.pi * n * k / 8)
+            im = im - g[n] * math.sin(math.pi * n * k / 8)
+        out[k] = (re, im)
+    return out
+
+
+def channelize_kernel(
+    first, x_ref, taps_ref, gain_ref, pair_ref, single_ref, out_ref, power_ref, y_hi, y_lo, spec
+):
+    step = pl.program_id(0)
+    tap_count = taps_ref.shape[0]
+    inputs = x_ref.shape[1]
+    groups, per_group = out_ref.shape[0], out_ref.shape[3]
+    row_tiles = inputs // 16
+
+    def filter_rows(index, carry):
+        frame = index // row_tiles
+        tile = index % row_tiles
+        rows = pl.ds(pl.multiple_of(tile * 16, 16), 16)
+        out_rows = pl.ds(pl.multiple_of(index * 16, 16), 16)
+        base = first + 2 * step + frame + tap_count - 1
+        for half in range(INNER // 128):
+            values = []
+            for block in range(OUTER):
+                lanes = pl.ds(block * INNER + half * 128, 128)
+                total = None
+                for tap in range(tap_count):
+                    sample = x_ref[base - tap, rows, lanes].astype(jnp.float32)
+                    term = sample.reshape(2, 8, 128) * taps_ref[tap, :, lanes]
+                    total = term if total is None else total + term
+                values.append(total.reshape(16, 128))
+            for k, both in real_dft16(values).items():
+                for part, value in enumerate(both):
+                    if value is None:
+                        continue
+                    slot = {0: 0, 8: 1}.get(k, 2 * k) + part
+                    lanes = pl.ds(slot * INNER + half * 128, 128)
+                    high = value.astype(jnp.bfloat16)
+                    y_hi[out_rows, lanes] = high
+                    y_lo[out_rows, lanes] = (value - high.astype(jnp.float32)).astype(jnp.bfloat16)
+        return carry
+
+    lax.fori_loop(0, 2 * row_tiles, filter_rows, 0)
+
+    def product(table, index, lanes):
+        high, low = y_hi[:, lanes], y_lo[:, lanes]
+        dot = functools.partial(
+            lax.dot_general, dimension_numbers=NT, preferred_element_type=jnp.float32
+        )
+        return dot(table[0, index], high) + (dot(table[1, index], high) + dot(table[0, index], low))
+
+    def spread(result, row, residue):
+        for part in range(2):
+            for frame in range(2):
+                first_row = row + part * (INNER // 2)
+                spec[2 * part + frame, pl.ds(residue, INNER // 2, stride=OUTER), :] = result[
+                    first_row : first_row + INNER // 2, frame * inputs : (frame + 1) * inputs
+                ]
+
+    for residue in range(1, OUTER // 2):
+        result = product(pair_ref, residue - 1, pl.ds(2 * residue * INNER, 2 * INNER))
+        spread(result, 0, residue)
+        spread(result, INNER, OUTER - residue)
+    for index, residue in enumerate((0, OUTER // 2)):
+        spread(product(single_ref, index, pl.ds(index * INNER, INNER)), 0, residue)
+
+    def finish(group, power):
+        rows = pl.ds(pl.multiple_of(group * per_group, per_group), per_group)
+        gain = gain_ref[rows, :]
+        for part in range(2):
+            for frame in range(2):
+                rounded = (spec[2 * part + frame, rows, :] * gain).astype(jnp.bfloat16)
+                out_ref[group, frame, part] = rounded
+                wide = rounded.astype(jnp.float32)
+                power = power + jnp.sum((wide * wide).reshape(per_group // 8, 8, inputs), axis=0)
+        return power
+
+    power_ref[0] = lax.fori_loop(0, groups, finish, jnp.zeros((8, inputs), jnp.float32))
+
+
+def channelize(extended, taps, gains, tables, first, frames, groups):
+    inputs, length = extended.shape[1:]
+    channels = gains.shape[0]
+    per_group = channels // groups
+    steps = frames // 2
+    whole = lambda array: pl.BlockSpec(
+        array.shape, lambda i: (0,) * array.ndim, pipeline_mode=pl.Buffered(1)
+    )
+    return pl.pallas_call(
+        functools.partial(channelize_kernel, first),
+        grid=(steps,),
+        in_specs=[whole(array) for array in (extended, taps, gains, *tables)],
+        out_specs=[
+            pl.BlockSpec((groups, 2, 2, per_group, inputs), lambda i: (0, i, 0, 0, 0)),
+            pl.BlockSpec((1, 8, inputs), lambda i: (i, 0, 0)),
+        ],
+        out_shape=[
+            jax.ShapeDtypeStruct((groups, frames, 2, per_group, inputs), jnp.bfloat16),
+            jax.ShapeDtypeStruct((steps, 8, inputs), jnp.float32),
+        ],
+        scratch_shapes=[
+            pltpu.VMEM((2 * inputs, length), jnp.bfloat16),
+            pltpu.VMEM((2 * inputs, length), jnp.bfloat16),
+            pltpu.VMEM((4, channels, inputs), jnp.float32),
+        ],
+        compiler_params=pltpu.CompilerParams(vmem_limit_bytes=62 * 2**20),
+        cost_estimate=pl.CostEstimate(
+            flops=frames * inputs * channels * 12000, bytes_accessed=60 * 2**20, transcendentals=0
+        ),
+        name="channelize",
+    )(extended, taps, gains, *tables)
+
+
+def correlate_kernel(stations, *refs):
+    *part_refs, weight_ref, out_ref, columns = refs
+    sub = pl.program_id(1)
+    sub_count = out_ref.shape[0]
+    half_frames = columns.shape[1] // 2
+    inputs = columns.shape[2]
+
+    @pl.when(sub == 0)
+    def _():
+        row = 0
+        for ref in part_refs:
+            times = ref.shape[0] // stations
+            frames, _, _, lanes = ref.shape[1:]
+
+            def turn(index, carry, ref=ref, row=row, times=times, frames=frames, lanes=lanes):
+                for station in range(stations):
+                    for part in range(2):
+                        block = ref[station * times + index, :, part].astype(jnp.float32)
+                        start = part * half_frames + row + index * frames
+                        columns[
+                            :,
+                            pl.ds(pl.multiple_of(start, 8), frames),
+                            station * lanes : (station + 1) * lanes,
+                        ] = jnp.transpose(block, (1, 0, 2))
+                return carry
+
+            lax.fori_loop(0, times, turn, 0)
+            row += times * frames
+
+    half = inputs // 2
+    dot = functools.partial(
+        lax.dot_general, dimension_numbers=TN, preferred_element_type=jnp.float32
+    )
+    lower = lax.broadcasted_iota(jnp.int32, (half, half), 0) >= lax.broadcasted_iota(
+        jnp.int32, (half, half), 1
+    )
+
+    def one(index, carry):
+        straight = columns[sub * sub_count + index].astype(jnp.bfloat16)
+        turned = jnp.concatenate([straight[half_frames:], -straight[:half_frames]], axis=0)
+        for row in range(2):
+            for col in range(2):
+                rows = slice(row * half, (row + 1) * half)
+                cols = slice(col * half, (col + 1) * half)
+                right = straight[:, cols]
+                if row > col:
+                    value = dot(straight[:, rows], right)
+                elif row < col:
+                    value = dot(turned[:, rows], right)
+                else:
+                    value = jnp.where(
+                        lower, dot(straight[:, rows], right), dot(turned[:, rows], right)
+                    )
+                out_ref[index, rows, cols] = value * weight_ref[rows, cols]
+        return carry
+
+    lax.fori_loop(0, sub_count, one, 0)
+
+
+def correlate(parts, weight, stations):
+    devices, _, _, per_group, lanes = parts[0].shape
+    inputs = stations * lanes
+    all_frames = sum(part.shape[1] for part in parts) * (devices // stations)
+    tile, sub = 16, 4
+    return pl.pallas_call(
+        functools.partial(correlate_kernel, stations),
+        grid=(per_group // tile, tile // sub),
+        in_specs=[
+            pl.BlockSpec((devices, part.shape[1], 2, tile, lanes), lambda i, j: (0, 0, 0, i, 0))
+            for part in parts
+        ]
+        + [pl.BlockSpec((inputs, inputs), lambda i, j: (0, 0))],
+        out_specs=pl.BlockSpec((sub, inputs, inputs), lambda i, j: (i * (tile // sub) + j, 0, 0)),
+        out_shape=jax.ShapeDtypeStruct((per_group, inputs, inputs), jnp.float32),
+        scratch_shapes=[pltpu.VMEM((tile, 2 * all_frames, inputs), jnp.float32)],
+        compiler_params=pltpu.CompilerParams(vmem_limit_bytes=56 * 2**20),
+        name="correlate",
+    )(*parts, weight)
+
+
+def per_device_tiled(voltages, pfb_taps, eq_gains):
+    tap_count, length = pfb_taps.shape
+    history_len = tap_count - 1
+    inputs_dev, frames_dev, _ = voltages.shape
+    channels = eq_gains.shape[1]
+    station_groups = lax.axis_size("stn")
+    time_groups = lax.axis_size("tm")
+    groups = station_groups * time_groups
+    all_inputs = inputs_dev * station_groups
+    all_frames = frames_dev * time_groups
+    frame_major = jnp.transpose(voltages, (1, 0, 2))
+    earlier = from_behind(frame_major[frames_dev - history_len :], "tm", 1)
+    extended = jnp.concatenate([earlier, frame_major], axis=0)
+    taps = jnp.broadcast_to(pfb_taps[:, None, :], (tap_count, 8, length))
+    gains = jnp.transpose(eq_gains)
+    tables = [jnp.asarray(table) for table in dft_tables(length)]
+    piece = frames_dev // PIECES
+    received, power = [], 0.0
+    for index in range(PIECES):
+        spectra, partial = channelize(
+            extended, taps, gains, tables, index * piece, piece, groups
+        )
+        received.append(
+            lax.all_to_all(spectra, ("stn", "tm"), split_axis=0, concat_axis=0, tiled=True)
+        )
+        power = power + jnp.sum(partial, axis=(0, 1))
+    placed = lax.dynamic_update_slice(
+        jnp.zeros((all_inputs,), jnp.float32), power, (lax.axis_index("stn") * inputs_dev,)
+    )
+    power = lax.psum(placed, ("stn", "tm"))
+    scale = lax.rsqrt(power / (all_frames * channels) + 1e-06)
+    weight = scale[:, None] * scale[None, :] / all_frames
+    return correlate(received, weight, station_groups)
+
+
+PIECES = 2
+
+
+def fits_tiles(mesh, voltages, pfb_taps, eq_gains):
+    inputs = voltages.shape[0] // mesh.shape["stn"]
+    frames = voltages.shape[1] // mesh.shape["tm"]
+    per_group = eq_gains.shape[1] // mesh.size
+    return (
+        voltages.shape[2] == OUTER * INNER
+        and 2 * eq_gains.shape[1] == voltages.shape[2]
+        and inputs == 128
+        and frames == 16
+        and pfb_taps.shape[0] == 16
+        and per_group % 16 == 0
+        and voltages.shape[:2] == (512, 128)
+    )
+
+
 def solution(mesh):
     in_specs = (P("stn", "tm", None), P(), P("stn", None))
     out_specs = P(("stn", "tm"), None, None)
-    return jax.shard_map(
-        per_device, mesh=mesh, in_specs=in_specs, out_specs=out_specs, check_vma=False
-    )
+
+    def run(voltages, pfb_taps, eq_gains):
+        body = per_device_tiled if fits_tiles(mesh, voltages, pfb_taps, eq_gains) else per_device
+        return jax.shard_map(
+            body, mesh=mesh, in_specs=in_specs, out_specs=out_specs, check_vma=False
+        )(voltages, pfb_taps, eq_gains)
+
+    return run

time: 1420 us -> 745 us (0.52)
  local copies, waits for them, and re-layouts: 601 us -> 28.3 us
  matrix products: 286 us -> 0 us
  Pallas kernels: 0 us -> 192 us
  waiting for transfers between devices: 455 us -> 280 us
  blocking collectives: 43.3 us -> 203 us
    all_to_all x1 -> x2, waiting for transfers between devices: 359 us -> 109 us  [per_device_tiled(): lax.all_to_all(spectra, ('stn', 'tm'), split_axis=0, concat_axis=0, tiled...]
    dot_general x5 -> x0, matrix products: 242 us -> none  [the longest x1 90.9 us: transform(): jnp.einsum('qjksb,skbR->qjkR', combined, partial_ft, precision=highest)]
    pallas_call x0 -> x3, Pallas kernels: none -> 192 us  [the longest x2 143 us: channelize(): pl.pallas_call(functools.partial(channelize_kernel, first), grid=(steps,)...]
    reshape x4 -> x0, local copies, waits for them, and re-layouts: 174 us -> none  [the longest x2 104 us: transform(): arranged = filtered.reshape(row_count, outer_len, inner_len)]
    psum x1, blocking collectives: 43.3 us -> 203 us  [per_device_tiled(): power = lax.psum(placed, ('stn', 'tm'))]
    dot_general x1 -> x0, local copies, waits for them, and re-layouts: 87.7 us -> none  [per_device(): jnp.einsum('rcnt,rcmt->cnm', columns, columns, preferred_element_type=jnp...]
    ppermute x1, waiting for transfers between devices: 95.6 us -> 170 us  [from_behind(): lax.ppermute(value, axis, [(source, source + steps) for source in range(f...]
    mul x3 -> x0, local copies, waits for them, and re-layouts: 61.9 us -> none  [per_device(): spectrum.reshape(2, channels, inputs_dev, frames_dev)]
  transfers between devices with their start and end apart: 2 -> 3, of which waited for: 2 -> 2; matrix products, arithmetic and copies ran while one was open for 6% -> 0% of each run, Pallas kernels for 0% -> 10%
where the time goes in v1:
time: 745 us; the launch traced here: 742 us
  waiting for transfers between devices  280 us (38%)
  blocking collectives  203 us (27%)
  Pallas kernels  192 us (26%)
  local copies, waits for them, and re-layouts  28.3 us (4%)
  other arithmetic  23.4 us (3%)
  starting transfers between devices  16 us (2%)
    psum x1, blocking collectives, per_device_tiled(): power = lax.psum(placed, ('stn', 'tm'))  203 us
    ppermute x1, waiting for transfers between devices, from_behind(): lax.ppermute(value, axis, [(source, source + steps) for source in range(f...  170 us
    pallas_call x2, Pallas kernels, channelize(): pl.pallas_call(functools.partial(channelize_kernel, first), grid=(steps,)...  143 us
    all_to_all x2, waiting for transfers between devices, per_device_tiled(): lax.all_to_all(spectra, ('stn', 'tm'), split_axis=0, concat_axis=0, tiled...  109 us
    pallas_call x1, Pallas kernels, correlate(): pl.pallas_call(functools.partial(correlate_kernel, stations), grid=(per_g...  49.5 us
    concatenate x1, other arithmetic, per_device_tiled(): extended = jnp.concatenate([earlier, frame_major], axis=0)  22.1 us
    unnamed x12, local copies, waits for them, and re-layouts  20.5 us
  transfers between devices with their start and end apart: 3, of which 2 were waited for; matrix products, arithmetic and copies ran while one was open for 0% of the time, Pallas kernels for 10%

profile of v1, /device:TPU:10, one launch (start us, length us, event | category | flops | bytes accessed | tf_op | source)
XLA Modules:
  0.0 742.1 jit_solution(13620711160281904390)
XLA Ops:
  0.0 14.7 %copy.9 = bf16[128,16,4096]{2,0,1:T(8,128)(2,1)S(1)} copy(bf16[128,16,4096]{2,1,0:T(8,128)(2,1)} %param.5) | data formatting | bytes 33554432 | tf_op args[0]
  14.7 0.0 copy-start
  14.7 0.0 copy-start.1
  14.7 6.2 slice.4
  21.0 4.4 copy-done
  25.4 1.9 collective-permute-start
  27.3 0.0 copy-done.1
  27.3 1.3 copy.7
  28.6 0.0 copy-start.2
  28.6 170.5 %collective-permute-done = bf16[15,128,4096]{2,1,0:T(8,128)(2,1)} collective-permute-done((bf16[15,128,4096]{2,1,0:T(8,128)(2,1)}, bf16[15,128,4096]{2,1,0:T(8,128)(2,1)}, u32[]{:S(2)}, u32[]{:S(2)}) %collective-permute-start) | collective-permute-done | bytes 15728672 | tf_op jit(solution)/shard_map/ppermute | solution.py:17
  199.1 22.1 %pad_maximum_fusion.x_ref = bf16[31,128,4096]{2,1,0:T(8,128)(2,1)} fusion(bf16[16,128,4096]{2,1,0:T(8,128)(2,1)} %bitcast.5, bf16[15,128,4096]{2,1,0:T(8,128)(2,1)} %collective-permute-done), kind=kLoop, calls=%fused_computation | loop fusion | flops 16252928 | bytes 65011712 | tf_op jit(solution)/shard_map/concatenate | solution.py:351
  221.2 0.0 copy-done.2
  221.2 1.6 broadcast_in_dim.4.taps_ref
  222.7 71.3 %channelize.3 = (bf16[32,8,2,64,128]{4,3,2,1,0:T(8,128)(2,1)}, f32[4,8,128]{2,1,0:T(8,128)}) custom-call(bf16[31,128,4096]{2,1,0:T(8,128)(2,1)} %pad_maximum_fusion.x_ref, f32[16,8,4096]{2,1,0:T(8,128)} %broadcast_in_dim.4.taps_ref, f32[2048,128]{1,0:T(8,128)} %bitcast.6, bf16[2,7,512,512]{3,2,1,0:T(8,128)(2,1)} %constant.26.clone.pair_ref, ...), custom_call_target="tpu_custom_call" | custom-call | flops 25165824000 | bytes 62914560 | tf_op jit(solution)/shard_map/channelize/pallas_call | solution.py:234
  294.0 6.1 all-to-all-start.1
  300.1 71.3 %channelize.2 = (bf16[32,8,2,64,128]{4,3,2,1,0:T(8,128)(2,1)}, f32[4,8,128]{2,1,0:T(8,128)}) custom-call(bf16[31,128,4096]{2,1,0:T(8,128)(2,1)} %pad_maximum_fusion.x_ref, f32[16,8,4096]{2,1,0:T(8,128)} %broadcast_in_dim.4.taps_ref, f32[2048,128]{1,0:T(8,128)} %bitcast.7, bf16[2,7,512,512]{3,2,1,0:T(8,128)(2,1)} %constant.26.clone.pair_ref, ...), custom_call_target="tpu_custom_call" | custom-call | flops 25165824000 | bytes 62914560 | tf_op jit(solution)/shard_map/channelize/pallas_call | solution.py:234
  371.5 0.0 copy-start.3
  371.5 0.0 copy-start.4
  371.5 109.2 %all-to-all-done.1.refs_1_ = bf16[32,8,2,64,128]{4,3,2,1,0:T(8,128)(2,1)} async-done(((bf16[32,8,2,64,128]{4,3,2,1,0:T(8,128)(2,1)}), bf16[32,8,2,64,128]{4,3,2,1,0:T(8,128)(2,1)}, u32[]{:S(2)}, u32[]{:S(2)}) %all-to-all-start.1) | async-done | bytes 8388640 | tf_op jit(solution)/shard_map/all_to_all | solution.py:362
  480.6 8.0 %all-to-all-start = ((bf16[32,8,2,64,128]{4,3,2,1,0:T(8,128)(2,1)}), bf16[32,8,2,64,128]{4,3,2,1,0:T(8,128)(2,1)}, u32[]{:S(2)}, u32[]{:S(2)}) async-start(bf16[32,8,2,64,128]{4,3,2,1,0:T(8,128)(2,1)} %get-tuple-element.9), calls=%async_computation | async-start | bytes 16777216 | tf_op jit(solution)/shard_map/all_to_all | solution.py:362
  488.7 0.0 copy-done.3
  488.7 0.0 copy-done.4
  488.7 0.1 add_dynamic-update-slice_fusion
  488.8 202.6 %psum.7 = f32[512]{0:T(512)S(1)} all-reduce(f32[512]{0:T(512)S(1)} %add_dynamic-update-slice_fusion), channel_id=1, replica_groups=mesh['stn'=4,'tm'=8] {'stn','tm'}, use_global_device_ids=true, to_apply=%region_2.0 | all-reduce | flops 512 | bytes 4096 | tf_op jit(solution)/shard_map/psum | solution.py:368
  691.4 1.2 multiply_multiply_fusion.refs_2_
  692.6 0.0 all-to-all-done.refs_0_
  692.6 49.5 %correlate.1 = f32[64,512,512]{2,1,0:T(8,128)} custom-call(bf16[32,8,2,64,128]{4,3,2,1,0:T(8,128)(2,1)} %all-to-all-done.refs_0_, bf16[32,8,2,64,128]{4,3,2,1,0:T(8,128)(2,1)} %all-to-all-done.1.refs_1_, f32[512,512]{1,0:T(8,128)} %multiply_multiply_fusion.refs_2_), custom_call_target="tpu_custom_call" | custom-call | tf_op jit(solution)/shard_map/correlate/pallas_call | solution.py:323
  (4 shorter events, 0.0 us)
Async XLA Ops:
  14.7 10.6 %copy-start = (bf16[128,16,4096]{2,0,1:T(8,128)(2,1)}, bf16[128,16,4096]{2,0,1:T(8,128)(2,1)S(1)}, u32[]{:S(2)}) copy-start(bf16[128,16,4096]{2,0,1:T(8,128)(2,1)S(1)} %copy.9) | copy-start | bytes 50331652
  14.7 12.6 %copy-start.1 = (f32[128,2048]{1,0:T(8,128)S(1)}, f32[128,2048]{1,0:T(8,128)}, u32[]{:S(2)}) copy-start(f32[128,2048]{1,0:T(8,128)} %param.7) | copy-start | bytes 3145732
  25.4 173.7 %collective-permute-start = (bf16[15,128,4096]{2,1,0:T(8,128)(2,1)}, bf16[15,128,4096]{2,1,0:T(8,128)(2,1)}, u32[]{:S(2)}, u32[]{:S(2)}) collective-permute-start(bf16[15,128,4096]{2,1,0:T(8,128)(2,1)} %slice.4), channel_id=1, source_target_pairs={{0,1},{1,2},{2,3},{3,4},{4,5},{5,6},{6,7},{8,9},{9,10},{10,11},{11... | collective-permute-start | bytes 47185928 | tf_op jit(solution)/shard_map/ppermute | solution.py:17
  28.6 192.5 %copy-start.2 = (f32[16,4096]{1,0:T(8,128)S(1)}, f32[16,4096]{1,0:T(8,128)}, u32[]{:S(2)}) copy-start(f32[16,4096]{1,0:T(8,128)} %param.6) | copy-start | bytes 786436
  294.0 186.6 %all-to-all-start.1 = ((bf16[32,8,2,64,128]{4,3,2,1,0:T(8,128)(2,1)}), bf16[32,8,2,64,128]{4,3,2,1,0:T(8,128)(2,1)}, u32[]{:S(2)}, u32[]{:S(2)}) async-start(bf16[32,8,2,64,128]{4,3,2,1,0:T(8,128)(2,1)} %get-tuple-element.10), calls=%async_computation.1 | async-start | bytes 16777216 | tf_op jit(solution)/shard_map/all_to_all | solution.py:362
  371.5 117.2 %copy-start.3 = (f32[4,8,128]{2,1,0:T(8,128)S(1)}, f32[4,8,128]{2,1,0:T(8,128)}, u32[]{:S(2)}) copy-start(f32[4,8,128]{2,1,0:T(8,128)} %get-tuple-element.12) | copy-start | bytes 49156
  371.5 117.2 %copy-start.4 = (f32[4,8,128]{2,1,0:T(8,128)S(1)}, f32[4,8,128]{2,1,0:T(8,128)}, u32[]{:S(2)}) copy-start(f32[4,8,128]{2,1,0:T(8,128)} %get-tuple-element.11) | copy-start | bytes 49156
  480.6 212.0 %all-to-all-start = ((bf16[32,8,2,64,128]{4,3,2,1,0:T(8,128)(2,1)}), bf16[32,8,2,64,128]{4,3,2,1,0:T(8,128)(2,1)}, u32[]{:S(2)}, u32[]{:S(2)}) async-start(bf16[32,8,2,64,128]{4,3,2,1,0:T(8,128)(2,1)} %get-tuple-element.9), calls=%async_computation | async-start | bytes 16777216 | tf_op jit(solution)/shard_map/all_to_all | solution.py:362
